TPU v7x, 32 devices: a whole 2x2x4 slice. The times are simulated.
32 devices in a mesh: lists: 16 (over z, x, core), sub: 2 (over y).
Axes of the slice: x: 2, y: 2, z: 4, core: 2. Of those that a mesh axis runs over, the one named last changes fastest.
Arguments:
- vectors: bfloat16 [768, 6144], P('sub', 'lists'), may hold values from -6 to 6
- list_ids: int32 [6144], P('lists'), may hold values from 0 to 63
- counts: int32 [16, 16], replicated, may hold values from 0 to 24, as said below
- coarse: bfloat16 [768, 1024], P(None, ('lists', 'sub')), may hold values from -3 to 3
- codebook_init: float32 [768, 256], P('sub'), may hold values from -6 to 6
- codes: int32 [2, 96, 6144], P(None, 'sub', 'lists'), may hold values from 0 to 255
Outputs:
- codebook: float32 [768, 256], P('sub')
- leftover: bfloat16 [768, 6144], P('sub', 'lists')
Inputs may be any that keep to these rules, and one draw needn't show every extreme that they name: `counts`: counts of used slots in each block; in every draw one owner receives full blocks of 24 from every sender. `list_ids`: every slot names one of its block owner's lists.
All inputs are finite; a program needn't handle non-finite values.
Results may differ from a plain program's by a relative error of at most 0.0051.
Values may be sent and summed in bfloat16 or wider, within the bound.
A program may use at most 64 MiB of HBM per device.

v0:
```python
import jax
import jax.numpy as jnp
from jax import lax
from jax.sharding import PartitionSpec as P

K = 256
DS = 8
LISTS_DEV = 64
ITERS = 2


def shards(vectors, list_ids, counts, coarse, codebook_init, codes):
    features, rows = vectors.shape
    owners = lax.axis_size("lists")
    owner = lax.axis_index("lists")
    block = rows // owners
    subspaces = features // DS
    mine = lax.all_to_all(coarse, "sub", split_axis=0, concat_axis=1, tiled=True)
    list_iota = jnp.arange(LISTS_DEV, dtype=jnp.int32)
    arrived = lax.all_to_all(vectors, "lists", split_axis=1, concat_axis=1, tiled=True)
    labels = lax.all_to_all(
        list_ids.reshape(1, rows), "lists", split_axis=1, concat_axis=1, tiled=True
    ).reshape(rows)
    selector = (labels[None, :] == list_iota[:, None]).astype(jnp.bfloat16)
    centre = jnp.dot(mine, selector, preferred_element_type=jnp.float32)
    residual = (arrived.astype(jnp.float32) - centre).astype(jnp.bfloat16)
    block_counts = lax.dynamic_index_in_dim(counts, owner, 1, keepdims=False)
    valid = (jnp.arange(block, dtype=jnp.int32)[None, :] < block_counts[:, None]).reshape(rows)
    code_iota = jnp.arange(K, dtype=jnp.int32)
    split_res = residual.reshape(subspaces, DS, rows)
    group_size = 4
    groups = subspaces // group_size
    grouped_res = split_res.reshape(groups, group_size, DS, rows)
    grouped_codes = jnp.swapaxes(codes, 0, 1).reshape(groups, group_size, ITERS, rows)

    def group_sums(packed):
        sub_res, sub_codes = packed
        one_hot = (sub_codes[:, :, None, :] == code_iota[None, None, :, None]) & valid[
            None, None, None, :
        ]
        one_hot = one_hot.astype(jnp.bfloat16)
        sums = jnp.einsum("gdr,gtkr->tgdk", sub_res, one_hot, preferred_element_type=jnp.float32)
        tally = jnp.swapaxes(jnp.sum(one_hot, axis=3, dtype=jnp.float32), 0, 1)
        return (sums, tally)

    part_sums, part_counts = lax.map(group_sums, (grouped_res, grouped_codes))
    part_sums = jnp.swapaxes(part_sums, 0, 1).reshape(ITERS, features, K)
    part_counts = jnp.swapaxes(part_counts, 0, 1).reshape(ITERS, subspaces, K)
    weight = 0.25 * jnp.sum(counts).astype(jnp.float32) / K
    total_sums, total_counts = lax.psum((part_sums, part_counts), "lists")
    codebook = codebook_init
    for iteration in range(ITERS):
        spread = jnp.repeat(total_counts[iteration], DS, axis=0)
        codebook = (total_sums[iteration] + weight * codebook) / (spread + weight)
    high = codebook.astype(jnp.bfloat16)
    low = (codebook - high.astype(jnp.float32)).astype(jnp.bfloat16)
    books = jnp.concatenate(
        [high.reshape(subspaces, DS, K), low.reshape(subspaces, DS, K)], axis=1
    ).reshape(groups, group_size, 2 * DS, K)

    def group_pick(packed):
        book, sub_codes = packed
        one_hot = (sub_codes[:, None, :] == code_iota[None, :, None]).astype(jnp.bfloat16)
        both = jnp.einsum("gdk,gkr->gdr", book, one_hot, preferred_element_type=jnp.float32)
        return both[:, :DS] + both[:, DS:]

    picked = lax.map(group_pick, (books, grouped_codes[:, :, ITERS - 1]))
    picked = picked.reshape(subspaces, DS, rows)
    leftover = jnp.where(valid[None, None, :], split_res.astype(jnp.float32) - picked, 0.0)
    leftover = leftover.astype(jnp.bfloat16).reshape(features, rows)
    return (codebook, leftover)


def solution(mesh):
    return jax.shard_map(
        shards,
        mesh=mesh,
        in_specs=(
            P("sub", "lists"),
            P("lists"),
            P(),
            P(None, ("lists", "sub")),
            P("sub", None),
            P(None, "sub", "lists"),
        ),
        out_specs=(P("sub", None), P("sub", "lists")),
        check_vma=False,
    )
```

profile of v0, /device:TPU:0, one launch (start us, length us, event | category | flops | bytes accessed | tf_op | source)
XLA Modules:
  0.0 176.7 jit_solution(4619838477152994786)
XLA Ops:
  7.2 1.4 all_to_all.28
  8.6 7.4 %all-to-all-start.1 = ((s32[1,16,24]{2,0,1:T(1,128)}), s32[1,16,24]{2,0,1:T(1,128)S(1)}, u32[]{:S(2)}, u32[]{:S(2)}) async-start(s32[1,16,24]{2,0,1:T(1,128)} %all_to_all.28), calls=%async_computation.1 | async-start | bytes 16384 | tf_op jit(solution)/shard_map/all_to_all | solution.py:21
  16.0 1.9 %copy.21 = bf16[384,384]{0,1:T(8,128)(2,1)} copy(bf16[384,384]{1,0:T(8,128)(2,1)} %param.10) | data formatting | bytes 589824 | tf_op args[0]
  17.8 4.5 %all-to-all-done.1 = s32[1,16,24]{2,0,1:T(1,128)S(1)} async-done(((s32[1,16,24]{2,0,1:T(1,128)}), s32[1,16,24]{2,0,1:T(1,128)S(1)}, u32[]{:S(2)}, u32[]{:S(2)}) %all-to-all-start.1) | async-done | bytes 1568 | tf_op jit(solution)/shard_map/all_to_all | solution.py:21
  22.3 3.5 %all-to-all-start = ((bf16[384,16,24]{0,2,1:T(8,128)(2,1)}), bf16[384,16,24]{0,2,1:T(8,128)(2,1)S(1)}, u32[]{:S(2)}, u32[]{:S(2)}) async-start(bf16[384,16,24]{0,2,1:T(8,128)(2,1)} %bitcast.1), calls=%async_computation | async-start | bytes 589824 | tf_op jit(solution)/shard_map/all_to_all | solution.py:20
  25.9 0.6 copy.36
  26.6 0.7 reduce_sum.18
  28.6 0.6 reduce.5
  29.4 7.0 %all-to-all-done = bf16[384,16,24]{0,2,1:T(8,128)(2,1)S(1)} async-done(((bf16[384,16,24]{0,2,1:T(8,128)(2,1)}), bf16[384,16,24]{0,2,1:T(8,128)(2,1)S(1)}, u32[]{:S(2)}, u32[]{:S(2)}) %all-to-all-start) | async-done | bytes 294944 | tf_op jit(solution)/shard_map/all_to_all | solution.py:20
  36.4 3.3 %all-to-all-start.2 = ((bf16[2,384,32]{1,2,0:T(8,128)(2,1)}), bf16[2,384,32]{1,2,0:T(8,128)(2,1)S(1)}, u32[]{:S(2)}, u32[]{:S(2)}) async-start(bf16[2,384,32]{1,2,0:T(8,128)(2,1)} %bitcast.93), calls=%async_computation.2 | async-start | bytes 98304 | tf_op jit(solution)/shard_map/all_to_all | solution.py:18
  40.0 3.7 %all-to-all-done.2 = bf16[2,384,32]{1,2,0:T(8,128)(2,1)S(1)} async-done(((bf16[2,384,32]{1,2,0:T(8,128)(2,1)}), bf16[2,384,32]{1,2,0:T(8,128)(2,1)S(1)}, u32[]{:S(2)}, u32[]{:S(2)}) %all-to-all-start.2) | async-done | bytes 49184 | tf_op jit(solution)/shard_map/all_to_all | solution.py:18
  44.0 25.4 %while.24 = (s32[]{:T(128)}, f32[12,2,4,8,256]{4,3,1,2,0:T(8,128)S(1)}, f32[12,2,4,256]{3,1,2,0:T(2,128)}, s32[12,4,2,384]{3,1,0,2:T(4,128)S(1)}, bf16[12,4,8,38...) while((s32[]{:T(128)}, f32[12,2,4,8,256]{4,3,1,2,0:T(8,128)S(1)}, ...), condition=%wide.region_2.3_spmd.clone, body=%wide.region_0.2_spmd.clone.sunk | while | flops 18086272 | bytes 192145 | solution.py:46
  44.2 0.7 fusion.48
  44.9 0.6 convert_reduce_fusion.2
  45.5 0.6 bitcast_dynamic-update-slice_fusion.2
  46.3 0.7 fusion.48
  47.0 0.6 convert_reduce_fusion.2
  47.6 0.6 bitcast_dynamic-update-slice_fusion.2
  48.4 0.7 fusion.48
  49.1 0.6 convert_reduce_fusion.2
  50.5 0.7 fusion.48
  51.2 0.6 convert_reduce_fusion.2
  52.6 0.7 fusion.48
  53.3 0.6 convert_reduce_fusion.2
  54.0 0.6 bitcast_dynamic-update-slice_fusion.2
  54.8 0.7 fusion.48
  55.4 0.6 convert_reduce_fusion.2
  56.1 0.6 bitcast_dynamic-update-slice_fusion.2
  56.9 0.7 fusion.48
  57.6 0.6 convert_reduce_fusion.2
  59.0 0.7 fusion.48
  59.7 0.6 convert_reduce_fusion.2
  61.1 0.7 fusion.48
  61.8 0.6 convert_reduce_fusion.2
  62.4 0.6 bitcast_dynamic-update-slice_fusion.2
  63.2 0.7 fusion.48
  63.9 0.6 convert_reduce_fusion.2
  64.5 0.6 bitcast_dynamic-update-slice_fusion.2
  65.3 0.7 fusion.48
  66.0 0.6 convert_reduce_fusion.2
  67.4 0.7 fusion.48
  68.1 0.6 convert_reduce_fusion.2
  69.4 1.0 copy.25
  70.6 90.5 %all-reduce.3.cloned.1.call-done = (f32[2,384,256]{2,1,0:T(8,128)}, f32[2,48,256]{2,0,1:T(2,128)}) async-done(((f32[2,384,256]{2,1,0:T(8,128)}, f32[2,48,256]{2,0,1:T(2,128)}), (f32[2,384,256]{2,1,0:T(8,128)}, f32[2,48,256]{2,0,1:T(2,128)})) %all-reduce.3.cloned.1.call-update) | async-done | bytes 884752 | tf_op jit(solution)/shard_map/psum | solution.py:50
  161.1 1.1 slice_add_fusion.2
  162.2 2.0 %subtract_convert_fusion = (bf16[384,256]{1,0:T(8,128)(2,1)S(1)}, bf16[384,256]{1,0:T(8,128)(2,1)S(1)}, f32[384,256]{1,0:T(8,128)}) fusion(f32[48,256]{1,0:T(8,128)S(1)} %get-tuple-element.147, f32[48,256]{1,0:T(8,128)S(1)} %get-tuple-element.148, f32[384,256]{1,0:T(8,128)S(1)} %copy-done, f32[2,384,256]{2,1,0:T(8,128)} %get-tuple-element.140, f32[]{:T(128)S(6)} %div.9), kind=kLoop, calls=%fused_computation.43 | loop fusion | flops 983040 | bytes 2064388 | tf_op jit(solution)/shard_map/convert_element_type | solution.py:56
  164.2 4.8 %while.25 = (s32[]{:T(128)}, f32[12,4,8,384]{3,2,1,0:T(8,128)S(1)}, bf16[12,4,16,256]{3,2,1,0:T(8,128)(2,1)S(1)}, s32[12,4,384]{2,1,0:T(4,128)S(1)}, s32[]{:T(128)}) while((s32[]{:T(128)}, f32[12,4,8,384]{3,2,1,0:T(8,128)S(1)}, bf16[12,4,16,256]{3,2,1,0:T(8,128)(2,1)S(1)}, s32[12,4,384]{2,1,0:T(4,128)S(1)}, s32[]{:T(128)}) %tuple.52), condition=%wide.region_7.8_spmd.clone, body=%wide.region_6.7_spmd.clone.sunk | while | flops 12988418 | bytes 297033 | solution.py:67
  169.0 0.8 fusion.31
  (115 shorter events, 12.1 us)
Async XLA Ops:
  7.2 18.7 %copy-start.2 = (bf16[768,32]{0,1:T(8,128)(2,1)S(1)}, bf16[768,32]{0,1:T(8,128)(2,1)}, u32[]{:S(2)}) copy-start(bf16[768,32]{0,1:T(8,128)(2,1)} %param.13) | copy-start | bytes 147460
  7.2 19.3 %copy-start.1 = (s32[2,48,384]{2,1,0:T(8,128)S(1)}, s32[2,48,384]{2,1,0:T(8,128)}, u32[]{:S(2)}) copy-start(s32[2,48,384]{2,1,0:T(8,128)} %param.15) | copy-start | bytes 442372
  8.6 13.7 %all-to-all-start.1 = ((s32[1,16,24]{2,0,1:T(1,128)}), s32[1,16,24]{2,0,1:T(1,128)S(1)}, u32[]{:S(2)}, u32[]{:S(2)}) async-start(s32[1,16,24]{2,0,1:T(1,128)} %all_to_all.28), calls=%async_computation.1 | async-start | bytes 16384 | tf_op jit(solution)/shard_map/all_to_all | solution.py:21
  16.0 10.6 %copy-start.3 = (s32[16,16]{1,0:T(8,128)S(1)}, s32[16,16]{1,0:T(8,128)}, u32[]{:S(2)}) copy-start(s32[16,16]{1,0:T(8,128)} %param.12) | copy-start | bytes 3076
  22.3 14.1 %all-to-all-start = ((bf16[384,16,24]{0,2,1:T(8,128)(2,1)}), bf16[384,16,24]{0,2,1:T(8,128)(2,1)S(1)}, u32[]{:S(2)}, u32[]{:S(2)}) async-start(bf16[384,16,24]{0,2,1:T(8,128)(2,1)} %bitcast.1), calls=%async_computation | async-start | bytes 589824 | tf_op jit(solution)/shard_map/all_to_all | solution.py:20
  36.4 7.3 %all-to-all-start.2 = ((bf16[2,384,32]{1,2,0:T(8,128)(2,1)}), bf16[2,384,32]{1,2,0:T(8,128)(2,1)S(1)}, u32[]{:S(2)}, u32[]{:S(2)}) async-start(bf16[2,384,32]{1,2,0:T(8,128)(2,1)} %bitcast.93), calls=%async_computation.2 | async-start | bytes 98304 | tf_op jit(solution)/shard_map/all_to_all | solution.py:18
  39.7 121.4 %all-reduce.3.cloned.1.call-start = ((), (), s32[]{:S(2)}) async-start(), calls=%async_computation.3 | async-start | bytes 1769472 | tf_op jit(solution)/shard_map/psum | solution.py:50
  70.3 91.8 %copy-start = (f32[384,256]{1,0:T(8,128)S(1)}, f32[384,256]{1,0:T(8,128)}, u32[]{:S(2)}) copy-start(f32[384,256]{1,0:T(8,128)} %param.14) | copy-start | bytes 1179652
Sparse Core Ops, SparseCore 0:
  70.5 90.5 all-reduce.2
where the time goes:
time: 177 us
  waiting for transfers between devices  106 us (60%)
  local copies, waits for them, and re-layouts  14.8 us (8%)
  between operations  14.8 us (8%)
  starting transfers between devices  14.2 us (8%)
  other arithmetic  13.8 us (8%)
  matrix products  12.8 us (7%)
    psum x1, waiting for transfers between devices, shards(): total_sums, total_counts = lax.psum((part_sums, part_counts), 'lists')  90.5 us
    dot_general x12, matrix products, group_sums(): jnp.einsum('gdr,gtkr->tgdk', sub_res, one_hot, preferred_element_type=jnp...  8.24 us
    reduce_sum x12, other arithmetic, group_sums(): tally = jnp.swapaxes(jnp.sum(one_hot, axis=3, dtype=jnp.float32), 0, 1)  7.52 us
    all_to_all x1, starting transfers between devices, shards(): lax.all_to_all(list_ids.reshape(1, rows), 'lists', split_axis=1, concat_a...  7.36 us
    dynamic_update_slice x12, local copies, waits for them, and re-layouts, shards(): part_sums, part_counts = lax.map(group_sums, (grouped_res, grouped_codes))  7.27 us
    all_to_all x1, waiting for transfers between devices, shards(): lax.all_to_all(vectors, 'lists', split_axis=1, concat_axis=1, tiled=True)  7 us
    all_to_all x1, waiting for transfers between devices, shards(): lax.all_to_all(list_ids.reshape(1, rows), 'lists', split_axis=1, concat_a...  4.47 us
    dot_general x12, matrix products, group_pick(): jnp.einsum('gdk,gkr->gdr', book, one_hot, preferred_element_type=jnp.floa...  4.29 us
  transfers between devices with their start and end apart: 4, of which 4 were waited for; matrix products, arithmetic and copies ran while one was open for 3% of the time, Pallas kernels for 0%

commit v1 on v0

--- a/solution.py
+++ b/solution.py
@@ -9,6 +9,30 @@
 ITERS = 2
 
 
+def in_blocks(value, dim, peers):
+    shape = value.shape
+    tiles = value.reshape(*shape[:dim], peers, shape[dim] // peers, *shape[dim + 1 :])
+    return jnp.moveaxis(tiles, dim, 0)
+
+
+def in_order(blocks, dim):
+    blocks = jnp.moveaxis(blocks, 0, dim)
+    shape = blocks.shape
+    return blocks.reshape(*shape[:dim], shape[dim] * shape[dim + 1], *shape[dim + 2 :])
+
+
+def rotated_exchange(x, axis, split_dim, concat_dim):
+    length, index = (lax.axis_size(axis), lax.axis_index(axis))
+    blocks = in_blocks(x, split_dim, length)
+    out = blocks
+    for step in range(1, length):
+        target, source = ((index + step) % length, (index - step) % length)
+        sent = lax.dynamic_index_in_dim(blocks, target, 0)
+        theirs = lax.ppermute(sent, axis, [(i, (i + step) % length) for i in range(length)])
+        out = lax.dynamic_update_slice_in_dim(out, theirs, source, axis=0)
+    return in_order(out, concat_dim)
+
+
 def shards(vectors, list_ids, counts, coarse, codebook_init, codes):
     features, rows = vectors.shape
     owners = lax.axis_size("lists")
@@ -17,7 +41,7 @@
     subspaces = features // DS
     mine = lax.all_to_all(coarse, "sub", split_axis=0, concat_axis=1, tiled=True)
     list_iota = jnp.arange(LISTS_DEV, dtype=jnp.int32)
-    arrived = lax.all_to_all(vectors, "lists", split_axis=1, concat_axis=1, tiled=True)
+    arrived = rotated_exchange(vectors, "lists", 1, 1)
     labels = lax.all_to_all(
         list_ids.reshape(1, rows), "lists", split_axis=1, concat_axis=1, tiled=True
     ).reshape(rows)

time: 177 us -> 187 us (1.056)
  starting transfers between devices: 14.2 us -> 30.4 us
  waiting for transfers between devices: 106 us -> 99.6 us
    ppermute x0 -> x15, starting transfers between devices: none -> 21.3 us  [rotated_exchange(): lax.ppermute(sent, axis, [(i, (i + step) % length) for i in range(length)])]
    all_to_all x1 -> x0, waiting for transfers between devices: 7 us -> none  [shards(): lax.all_to_all(vectors, 'lists', split_axis=1, concat_axis=1, tiled=True)]
    psum x1, waiting for transfers between devices: 90.5 us -> 94.4 us  [shards(): total_sums, total_counts = lax.psum((part_sums, part_counts), 'lists')]
    all_to_all x1, waiting for transfers between devices: 3.66 us -> 0.01 us  [shards(): lax.all_to_all(coarse, 'sub', split_axis=0, concat_axis=1, tiled=True)]
    all_to_all x1 -> x0, starting transfers between devices: 3.54 us -> none  [shards(): lax.all_to_all(vectors, 'lists', split_axis=1, concat_axis=1, tiled=True)]
  transfers between devices with their start and end apart: 4 -> 18, of which waited for: 4 -> 4; matrix products, arithmetic and copies ran while one was open for 3% -> 2% of each run, Pallas kernels for 0% -> 0%
where the time goes in v1:
time: 187 us; the launch traced here: 186 us
  waiting for transfers between devices  99.6 us (53%)
  starting transfers between devices  30.4 us (16%)
  between operations  15.6 us (8%)
  other arithmetic  13.8 us (7%)
  local copies, waits for them, and re-layouts  13.7 us (7%)
  matrix products  12.8 us (7%)
    psum x1, waiting for transfers between devices, shards(): total_sums, total_counts = lax.psum((part_sums, part_counts), 'lists')  94.4 us
    ppermute x15, starting transfers between devices, rotated_exchange(): lax.ppermute(sent, axis, [(i, (i + step) % length) for i in range(length)])  21.3 us
    dot_general x12, matrix products, group_sums(): jnp.einsum('gdr,gtkr->tgdk', sub_res, one_hot, preferred_element_type=jnp...  8.24 us
    reduce_sum x12, other arithmetic, group_sums(): tally = jnp.swapaxes(jnp.sum(one_hot, axis=3, dtype=jnp.float32), 0, 1)  7.52 us
    dynamic_update_slice x12, local copies, waits for them, and re-layouts, shards(): part_sums, part_counts = lax.map(group_sums, (grouped_res, grouped_codes))  7.27 us
    all_to_all x1, starting transfers between devices, shards(): lax.all_to_all(list_ids.reshape(1, rows), 'lists', split_axis=1, concat_a...  5.76 us
    dot_general x12, matrix products, group_pick(): jnp.einsum('gdk,gkr->gdr', book, one_hot, preferred_element_type=jnp.floa...  4.29 us
    all_to_all x1, waiting for transfers between devices, shards(): lax.all_to_all(list_ids.reshape(1, rows), 'lists', split_axis=1, concat_a...  3.8 us
  transfers between devices with their start and end apart: 18, of which 4 were waited for; matrix products, arithmetic and copies ran while one was open for 2% of the time, Pallas kernels for 0%

profile of v1, /device:TPU:0, one launch (start us, length us, event | category | flops | bytes accessed | tf_op | source)
XLA Modules:
  0.0 186.4 jit_solution(12549656879039960394)
XLA Ops:
  7.4 1.2 copy.21
  9.3 2.6 %collective-permute-start.1 = (bf16[1,384,24]{1,2,0:T(8,128)(2,1)S(1)}, bf16[1,384,24]{1,2,0:T(8,128)(2,1)S(1)}, u32[]{:S(2)}, u32[]{:S(2)}) collective-permute-start(bf16[1,384,24]{1,2,0:T(8,128)(2,1)S(1)} %get-tuple-element.158), channel_id=1, source_target_pairs={{0,4},{2,6},{4,8},{6,10},{8,12},{10,14},{12,16},{14,18},{16,20},{1... | collective-permute-start | bytes 55304 | tf_op jit(solution)/shard_map/ppermute | solution.py:31
  11.8 2.4 %collective-permute-start.2 = (bf16[1,384,24]{1,2,0:T(8,128)(2,1)S(1)}, bf16[1,384,24]{1,2,0:T(8,128)(2,1)S(1)}, u32[]{:S(2)}, u32[]{:S(2)}) collective-permute-start(bf16[1,384,24]{1,2,0:T(8,128)(2,1)S(1)} %get-tuple-element.157), channel_id=1, source_target_pairs={{0,6},{2,8},{4,10},{6,12},{8,14},{10,16},{12,18},{14,20},{16,22},{... | collective-permute-start | bytes 55304 | tf_op jit(solution)/shard_map/ppermute | solution.py:31
  14.2 1.6 collective-permute-start.3
  16.0 0.7 all_to_all.20
  16.7 5.8 %all-to-all-start = ((s32[1,16,24]{2,0,1:T(1,128)}), s32[1,16,24]{2,0,1:T(1,128)S(1)}, u32[]{:S(2)}, u32[]{:S(2)}) async-start(s32[1,16,24]{2,0,1:T(1,128)} %all_to_all.20), calls=%async_computation | async-start | bytes 16384 | tf_op jit(solution)/shard_map/all_to_all | solution.py:45
  23.5 0.7 reduce_sum.18
  25.1 3.8 %all-to-all-done = s32[1,16,24]{2,0,1:T(1,128)S(1)} async-done(((s32[1,16,24]{2,0,1:T(1,128)}), s32[1,16,24]{2,0,1:T(1,128)S(1)}, u32[]{:S(2)}, u32[]{:S(2)}) %all-to-all-start) | async-done | bytes 1568 | tf_op jit(solution)/shard_map/all_to_all | solution.py:45
  28.9 3.3 %all-to-all-start.1 = ((bf16[2,384,32]{1,2,0:T(8,128)(2,1)}), bf16[2,384,32]{1,2,0:T(8,128)(2,1)S(1)}, u32[]{:S(2)}, u32[]{:S(2)}) async-start(bf16[2,384,32]{1,2,0:T(8,128)(2,1)} %bitcast.121), calls=%async_computation.1 | async-start | bytes 98304 | tf_op jit(solution)/shard_map/all_to_all | solution.py:42
  34.0 0.7 collective-permute-start.6
  34.7 2.4 %collective-permute-start.7 = (bf16[1,384,24]{1,2,0:T(8,128)(2,1)S(1)}, bf16[1,384,24]{1,2,0:T(8,128)(2,1)S(1)}, u32[]{:S(2)}, u32[]{:S(2)}) collective-permute-start(bf16[1,384,24]{1,2,0:T(8,128)(2,1)S(1)} %get-tuple-element.152), channel_id=1, source_target_pairs={{0,16},{2,18},{4,20},{6,22},{8,24},{10,26},{12,28},{14,30},{16,0},... | collective-permute-start | bytes 55304 | tf_op jit(solution)/shard_map/ppermute | solution.py:31
  37.2 3.2 %collective-permute-start.9 = (bf16[1,384,24]{1,2,0:T(8,128)(2,1)S(1)}, bf16[1,384,24]{1,2,0:T(8,128)(2,1)S(1)}, u32[]{:S(2)}, u32[]{:S(2)}) collective-permute-start(bf16[1,384,24]{1,2,0:T(8,128)(2,1)S(1)} %get-tuple-element.150), channel_id=1, source_target_pairs={{0,20},{2,22},{4,24},{6,26},{8,28},{10,30},{12,0},{14,2},{16,4},{1... | collective-permute-start | bytes 55304 | tf_op jit(solution)/shard_map/ppermute | solution.py:31
  40.4 2.5 %collective-permute-start.10 = (bf16[1,384,24]{1,2,0:T(8,128)(2,1)S(1)}, bf16[1,384,24]{1,2,0:T(8,128)(2,1)S(1)}, u32[]{:S(2)}, u32[]{:S(2)}) collective-permute-start(bf16[1,384,24]{1,2,0:T(8,128)(2,1)S(1)} %get-tuple-element.149), channel_id=1, source_target_pairs={{0,22},{2,24},{4,26},{6,28},{8,30},{10,0},{12,2},{14,4},{16,6},{18... | collective-permute-start | bytes 55304 | tf_op jit(solution)/shard_map/ppermute | solution.py:31
  43.0 1.2 collective-permute-start.12
  44.3 1.5 collective-permute-start.13
  45.7 1.9 %collective-permute-start.14 = (bf16[1,384,24]{1,2,0:T(8,128)(2,1)S(1)}, bf16[1,384,24]{1,2,0:T(8,128)(2,1)S(1)}, u32[]{:S(2)}, u32[]{:S(2)}) collective-permute-start(bf16[1,384,24]{1,2,0:T(8,128)(2,1)S(1)} %get-tuple-element.145), channel_id=1, source_target_pairs={{0,30},{2,0},{4,2},{6,4},{8,6},{10,8},{12,10},{14,12},{16,14},{18,... | collective-permute-start | bytes 55304 | tf_op jit(solution)/shard_map/ppermute | solution.py:31
  48.1 1.0 collective-permute-done.14
  49.7 25.4 %while.24 = (s32[]{:T(128)}, f32[12,2,4,8,256]{4,3,1,2,0:T(8,128)S(1)}, f32[12,2,4,256]{3,1,2,0:T(2,128)}, s32[12,4,2,384]{3,1,0,2:T(4,128)S(1)}, bf16[12,4,8,38...) while((s32[]{:T(128)}, f32[12,2,4,8,256]{4,3,1,2,0:T(8,128)S(1)}, ...), condition=%wide.region_2.3_spmd.clone, body=%wide.region_0.2_spmd.clone.sunk | while | flops 18086272 | bytes 192145 | solution.py:70
  49.9 0.7 fusion.46
  50.6 0.6 convert_reduce_fusion.2
  52.1 0.7 fusion.46
  52.7 0.6 convert_reduce_fusion.2
  54.2 0.7 fusion.46
  54.9 0.6 convert_reduce_fusion.2
  56.3 0.7 fusion.46
  57.0 0.6 convert_reduce_fusion.2
  58.4 0.7 fusion.46
  59.1 0.6 convert_reduce_fusion.2
  60.5 0.7 fusion.46
  61.2 0.6 convert_reduce_fusion.2
  62.6 0.7 fusion.46
  63.3 0.6 convert_reduce_fusion.2
  64.7 0.7 fusion.46
  65.4 0.6 convert_reduce_fusion.2
  66.8 0.7 fusion.46
  67.5 0.6 convert_reduce_fusion.2
  69.0 0.7 fusion.46
  69.6 0.6 convert_reduce_fusion.2
  71.1 0.7 fusion.46
  71.8 0.6 convert_reduce_fusion.2
  73.2 0.7 fusion.46
  73.9 0.6 convert_reduce_fusion.2
  75.1 1.0 copy.25
  76.3 94.4 %all-reduce.3.cloned.1.call-done = (f32[2,384,256]{2,1,0:T(8,128)}, f32[2,48,256]{2,0,1:T(2,128)}) async-done(((f32[2,384,256]{2,1,0:T(8,128)}, f32[2,48,256]{2,0,1:T(2,128)}), (f32[2,384,256]{2,1,0:T(8,128)}, f32[2,48,256]{2,0,1:T(2,128)})) %all-reduce.3.cloned.1.call-update) | async-done | bytes 884752 | tf_op jit(solution)/shard_map/psum | solution.py:74
  170.8 1.1 slice_add_fusion.2
  171.9 2.0 %subtract_convert_fusion.1 = (bf16[384,256]{1,0:T(8,128)(2,1)S(1)}, bf16[384,256]{1,0:T(8,128)(2,1)S(1)}, f32[384,256]{1,0:T(8,128)}) fusion(f32[48,256]{1,0:T(8,128)S(1)} %get-tuple-element.162, f32[48,256]{1,0:T(8,128)S(1)} %get-tuple-element.163, f32[384,256]{1,0:T(8,128)S(1)} %copy-done, f32[2,384,256]{2,1,0:T(8,128)} %get-tuple-element.140, f32[]{:T(128)S(6)} %div.9), kind=kLoop, calls=%fused_computation.42 | loop fusion | flops 983040 | bytes 2064388 | tf_op jit(solution)/shard_map/convert_element_type | solution.py:80
  173.9 4.8 %while.25 = (s32[]{:T(128)}, f32[12,4,8,384]{3,2,1,0:T(8,128)S(1)}, bf16[12,4,16,256]{3,2,1,0:T(8,128)(2,1)S(1)}, s32[12,4,384]{2,1,0:T(4,128)S(1)}, s32[]{:T(128)}) while((s32[]{:T(128)}, f32[12,4,8,384]{3,2,1,0:T(8,128)S(1)}, bf16[12,4,16,256]{3,2,1,0:T(8,128)(2,1)S(1)}, s32[12,4,384]{2,1,0:T(4,128)S(1)}, s32[]{:T(128)}) %tuple.66), condition=%wide.region_7.8_spmd.clone, body=%wide.region_6.7_spmd.clone.sunk | while | flops 12988418 | bytes 297033 | solution.py:91
  178.7 0.8 fusion.29
  (162 shorter events, 18.9 us)
Async XLA Ops:
  7.2 8.8 %copy-start.4 = (s32[384]{0:T(512)S(1)}, s32[384]{0:T(512)}, u32[]{:S(2)}) copy-start(s32[384]{0:T(512)} %param.11) | copy-start | bytes 4612
  7.4 15.4 %copy-start.2 = (bf16[768,32]{0,1:T(8,128)(2,1)S(1)}, bf16[768,32]{0,1:T(8,128)(2,1)}, u32[]{:S(2)}) copy-start(bf16[768,32]{0,1:T(8,128)(2,1)} %param.13) | copy-start | bytes 147460
  7.4 16.1 %copy-start.1 = (s32[2,48,384]{2,1,0:T(8,128)S(1)}, s32[2,48,384]{2,1,0:T(8,128)}, u32[]{:S(2)}) copy-start(s32[2,48,384]{2,1,0:T(8,128)} %param.15) | copy-start | bytes 442372
  8.6 14.9 %copy-start.3 = (s32[16,16]{1,0:T(8,128)S(1)}, s32[16,16]{1,0:T(8,128)}, u32[]{:S(2)}) copy-start(s32[16,16]{1,0:T(8,128)} %param.12) | copy-start | bytes 3076
  8.8 24.6 %collective-permute-start = (bf16[1,384,24]{1,2,0:T(8,128)(2,1)S(1)}, bf16[1,384,24]{1,2,0:T(8,128)(2,1)S(1)}, u32[]{:S(2)}, u32[]{:S(2)}) collective-permute-start(bf16[1,384,24]{1,2,0:T(8,128)(2,1)S(1)} %get-tuple-element.159), channel_id=1, source_target_pairs={{0,2},{2,4},{4,6},{6,8},{8,10},{10,12},{12,14},{14,16},{16,18},{18... | collective-permute-start | bytes 55304 | tf_op jit(solution)/shard_map/ppermute | solution.py:31
  9.3 24.7 %collective-permute-start.1 = (bf16[1,384,24]{1,2,0:T(8,128)(2,1)S(1)}, bf16[1,384,24]{1,2,0:T(8,128)(2,1)S(1)}, u32[]{:S(2)}, u32[]{:S(2)}) collective-permute-start(bf16[1,384,24]{1,2,0:T(8,128)(2,1)S(1)} %get-tuple-element.158), channel_id=1, source_target_pairs={{0,4},{2,6},{4,8},{6,10},{8,12},{10,14},{12,16},{14,18},{16,20},{1... | collective-permute-start | bytes 55304 | tf_op jit(solution)/shard_map/ppermute | solution.py:31
  11.8 22.9 %collective-permute-start.2 = (bf16[1,384,24]{1,2,0:T(8,128)(2,1)S(1)}, bf16[1,384,24]{1,2,0:T(8,128)(2,1)S(1)}, u32[]{:S(2)}, u32[]{:S(2)}) collective-permute-start(bf16[1,384,24]{1,2,0:T(8,128)(2,1)S(1)} %get-tuple-element.157), channel_id=1, source_target_pairs={{0,6},{2,8},{4,10},{6,12},{8,14},{10,16},{12,18},{14,20},{16,22},{... | collective-permute-start | bytes 55304 | tf_op jit(solution)/shard_map/ppermute | solution.py:31
  14.2 22.9 %collective-permute-start.3 = (bf16[1,384,24]{1,2,0:T(8,128)(2,1)S(1)}, bf16[1,384,24]{1,2,0:T(8,128)(2,1)S(1)}, u32[]{:S(2)}, u32[]{:S(2)}) collective-permute-start(bf16[1,384,24]{1,2,0:T(8,128)(2,1)S(1)} %get-tuple-element.156), channel_id=1, source_target_pairs={{0,8},{2,10},{4,12},{6,14},{8,16},{10,18},{12,20},{14,22},{16,24},... | collective-permute-start | bytes 55304 | tf_op jit(solution)/shard_map/ppermute | solution.py:31
  15.8 21.4 %collective-permute-start.4 = (bf16[1,384,24]{1,2,0:T(8,128)(2,1)S(1)}, bf16[1,384,24]{1,2,0:T(8,128)(2,1)S(1)}, u32[]{:S(2)}, u32[]{:S(2)}) collective-permute-start(bf16[1,384,24]{1,2,0:T(8,128)(2,1)S(1)} %get-tuple-element.155), channel_id=1, source_target_pairs={{0,10},{2,12},{4,14},{6,16},{8,18},{10,20},{12,22},{14,24},{16,26}... | collective-permute-start | bytes 55304 | tf_op jit(solution)/shard_map/ppermute | solution.py:31
  16.7 12.2 %all-to-all-start = ((s32[1,16,24]{2,0,1:T(1,128)}), s32[1,16,24]{2,0,1:T(1,128)S(1)}, u32[]{:S(2)}, u32[]{:S(2)}) async-start(s32[1,16,24]{2,0,1:T(1,128)} %all_to_all.20), calls=%async_computation | async-start | bytes 16384 | tf_op jit(solution)/shard_map/all_to_all | solution.py:45
  28.9 20.5 %all-to-all-start.1 = ((bf16[2,384,32]{1,2,0:T(8,128)(2,1)}), bf16[2,384,32]{1,2,0:T(8,128)(2,1)S(1)}, u32[]{:S(2)}, u32[]{:S(2)}) async-start(bf16[2,384,32]{1,2,0:T(8,128)(2,1)} %bitcast.121), calls=%async_computation.1 | async-start | bytes 98304 | tf_op jit(solution)/shard_map/all_to_all | solution.py:42
  32.1 138.6 %all-reduce.3.cloned.1.call-start = ((), (), s32[]{:S(2)}) async-start(), calls=%async_computation.2 | async-start | bytes 1769472 | tf_op jit(solution)/shard_map/psum | solution.py:74
  33.4 7.0 %collective-permute-start.5 = (bf16[1,384,24]{1,2,0:T(8,128)(2,1)S(1)}, bf16[1,384,24]{1,2,0:T(8,128)(2,1)S(1)}, u32[]{:S(2)}, u32[]{:S(2)}) collective-permute-start(bf16[1,384,24]{1,2,0:T(8,128)(2,1)S(1)} %get-tuple-element.154), channel_id=1, source_target_pairs={{0,12},{2,14},{4,16},{6,18},{8,20},{10,22},{12,24},{14,26},{16,28}... | collective-permute-start | bytes 55304 | tf_op jit(solution)/shard_map/ppermute | solution.py:31
  34.0 8.9 %collective-permute-start.6 = (bf16[1,384,24]{1,2,0:T(8,128)(2,1)S(1)}, bf16[1,384,24]{1,2,0:T(8,128)(2,1)S(1)}, u32[]{:S(2)}, u32[]{:S(2)}) collective-permute-start(bf16[1,384,24]{1,2,0:T(8,128)(2,1)S(1)} %get-tuple-element.153), channel_id=1, source_target_pairs={{0,14},{2,16},{4,18},{6,20},{8,22},{10,24},{12,26},{14,28},{16,30}... | collective-permute-start | bytes 55304 | tf_op jit(solution)/shard_map/ppermute | solution.py:31
  34.7 8.3 %collective-permute-start.7 = (bf16[1,384,24]{1,2,0:T(8,128)(2,1)S(1)}, bf16[1,384,24]{1,2,0:T(8,128)(2,1)S(1)}, u32[]{:S(2)}, u32[]{:S(2)}) collective-permute-start(bf16[1,384,24]{1,2,0:T(8,128)(2,1)S(1)} %get-tuple-element.152), channel_id=1, source_target_pairs={{0,16},{2,18},{4,20},{6,22},{8,24},{10,26},{12,28},{14,30},{16,0},... | collective-permute-start | bytes 55304 | tf_op jit(solution)/shard_map/ppermute | solution.py:31
  37.1 7.1 %collective-permute-start.8 = (bf16[1,384,24]{1,2,0:T(8,128)(2,1)S(1)}, bf16[1,384,24]{1,2,0:T(8,128)(2,1)S(1)}, u32[]{:S(2)}, u32[]{:S(2)}) collective-permute-start(bf16[1,384,24]{1,2,0:T(8,128)(2,1)S(1)} %get-tuple-element.151), channel_id=1, source_target_pairs={{0,18},{2,20},{4,22},{6,24},{8,26},{10,28},{12,30},{14,0},{16,2},{... | collective-permute-start | bytes 55304 | tf_op jit(solution)/shard_map/ppermute | solution.py:31
  37.2 8.5 %collective-permute-start.9 = (bf16[1,384,24]{1,2,0:T(8,128)(2,1)S(1)}, bf16[1,384,24]{1,2,0:T(8,128)(2,1)S(1)}, u32[]{:S(2)}, u32[]{:S(2)}) collective-permute-start(bf16[1,384,24]{1,2,0:T(8,128)(2,1)S(1)} %get-tuple-element.150), channel_id=1, source_target_pairs={{0,20},{2,22},{4,24},{6,26},{8,28},{10,30},{12,0},{14,2},{16,4},{1... | collective-permute-start | bytes 55304 | tf_op jit(solution)/shard_map/ppermute | solution.py:31
  40.4 7.2 %collective-permute-start.10 = (bf16[1,384,24]{1,2,0:T(8,128)(2,1)S(1)}, bf16[1,384,24]{1,2,0:T(8,128)(2,1)S(1)}, u32[]{:S(2)}, u32[]{:S(2)}) collective-permute-start(bf16[1,384,24]{1,2,0:T(8,128)(2,1)S(1)} %get-tuple-element.149), channel_id=1, source_target_pairs={{0,22},{2,24},{4,26},{6,28},{8,30},{10,0},{12,2},{14,4},{16,6},{18... | collective-permute-start | bytes 55304 | tf_op jit(solution)/shard_map/ppermute | solution.py:31
  42.9 4.7 %collective-permute-start.11 = (bf16[1,384,24]{1,2,0:T(8,128)(2,1)S(1)}, bf16[1,384,24]{1,2,0:T(8,128)(2,1)S(1)}, u32[]{:S(2)}, u32[]{:S(2)}) collective-permute-start(bf16[1,384,24]{1,2,0:T(8,128)(2,1)S(1)} %get-tuple-element.148), channel_id=1, source_target_pairs={{0,24},{2,26},{4,28},{6,30},{8,0},{10,2},{12,4},{14,6},{16,8},{18,... | collective-permute-start | bytes 55304 | tf_op jit(solution)/shard_map/ppermute | solution.py:31
  43.0 4.6 %collective-permute-start.12 = (bf16[1,384,24]{1,2,0:T(8,128)(2,1)S(1)}, bf16[1,384,24]{1,2,0:T(8,128)(2,1)S(1)}, u32[]{:S(2)}, u32[]{:S(2)}) collective-permute-start(bf16[1,384,24]{1,2,0:T(8,128)(2,1)S(1)} %get-tuple-element.147), channel_id=1, source_target_pairs={{0,26},{2,28},{4,30},{6,0},{8,2},{10,4},{12,6},{14,8},{16,10},{18,... | collective-permute-start | bytes 55304 | tf_op jit(solution)/shard_map/ppermute | solution.py:31
  44.3 3.8 %collective-permute-start.13 = (bf16[1,384,24]{1,2,0:T(8,128)(2,1)S(1)}, bf16[1,384,24]{1,2,0:T(8,128)(2,1)S(1)}, u32[]{:S(2)}, u32[]{:S(2)}) collective-permute-start(bf16[1,384,24]{1,2,0:T(8,128)(2,1)S(1)} %get-tuple-element.146), channel_id=1, source_target_pairs={{0,28},{2,30},{4,0},{6,2},{8,4},{10,6},{12,8},{14,10},{16,12},{18,... | collective-permute-start | bytes 55304 | tf_op jit(solution)/shard_map/ppermute | solution.py:31
  45.7 3.3 %collective-permute-start.14 = (bf16[1,384,24]{1,2,0:T(8,128)(2,1)S(1)}, bf16[1,384,24]{1,2,0:T(8,128)(2,1)S(1)}, u32[]{:S(2)}, u32[]{:S(2)}) collective-permute-start(bf16[1,384,24]{1,2,0:T(8,128)(2,1)S(1)} %get-tuple-element.145), channel_id=1, source_target_pairs={{0,30},{2,0},{4,2},{6,4},{8,6},{10,8},{12,10},{14,12},{16,14},{18,... | collective-permute-start | bytes 55304 | tf_op jit(solution)/shard_map/ppermute | solution.py:31
  76.1 95.7 %copy-start = (f32[384,256]{1,0:T(8,128)S(1)}, f32[384,256]{1,0:T(8,128)}, u32[]{:S(2)}) copy-start(f32[384,256]{1,0:T(8,128)} %param.14) | copy-start | bytes 1179652
Sparse Core Ops, SparseCore 0:
  76.3 94.4 all-reduce.2
